TPU v7x, 256 devices: a whole 4x4x8 slice. The times are simulated.
256 devices in a mesh: row: 64 (over y, x_hi, z), ch: 4 (over x_lo, core).
Axes of the slice: x: 4 (x_hi: 2, x_lo: 2; x = x_hi * 2 + x_lo), y: 4, z: 8, core: 2. Of those that a mesh axis runs over, the one named last changes fastest.
Arguments:
- pair_field: bfloat16 [128, 512, 512], P('ch', 'row'), may hold values from -25 to 25
- input_gain: float32 [128], replicated, may hold values from 0.5 to 1.5
- input_bias: float32 [128], replicated, may hold values from -1.2 to 1.2
- left_weight: bfloat16 [128, 128], P(None, 'ch'), may hold values from -0.5 to 0.5
- left_gate: bfloat16 [128, 128], P(None, 'ch'), may hold values from -0.5 to 0.5
- right_weight: bfloat16 [128, 128], P(None, 'ch'), may hold values from -0.5 to 0.5
- right_gate: bfloat16 [128, 128], P(None, 'ch'), may hold values from -0.5 to 0.5
- gate_weight: bfloat16 [128, 128], P(None, 'ch'), may hold values from -0.5 to 0.5
- output_gain: float32 [128], replicated, may hold values from 0.5 to 1.5
- output_bias: float32 [128], replicated, may hold values from -1.2 to 1.2
- final_weight: bfloat16 [128, 128], P(None, 'ch'), may hold values from -0.5 to 0.5
Outputs:
- transposed: bfloat16 [128, 512, 512], P('ch', 'row')
All inputs are finite; a program needn't handle non-finite values.
Results may differ from a plain program's by a relative error of at most 0.012.
Values may be sent and summed in bfloat16 or wider, within the bound.
No kernel may reach another device: no remote copies, remote signals or barrier semaphores. Data moves between devices by JAX's collectives and lax.ppermute only.
A program may use at most 64 MiB of HBM per device.

v0:
```python
import jax
import jax.numpy as jnp
from jax import lax
from jax.sharding import PartitionSpec as P

epsilon = 1e-05


def layer_norm(values, gain, bias):
    average = jnp.mean(values, axis=-2, keepdims=True)
    centred = values - average
    variance = jnp.mean(centred * centred, axis=-2, keepdims=True)
    return centred * lax.rsqrt(variance + epsilon) * gain[:, None] + bias[:, None]


def swap(array, step):
    return lax.ppermute(array, "ch", [(s, s ^ step) for s in range(4)])


def place(blocks, mine):
    stacked = jnp.stack(blocks)
    return jnp.stack([lax.dynamic_index_in_dim(stacked, mine ^ t, 0, False) for t in range(4)])


def body(
    pair_field,
    input_gain,
    input_bias,
    left_weight,
    left_gate,
    right_weight,
    right_gate,
    gate_weight,
    output_gain,
    output_bias,
    final_weight,
):
    mine = lax.axis_index("ch")
    core = mine % 2
    everyone = ("row", "ch")
    weights = jnp.concatenate(
        [w.T for w in (left_weight, left_gate, right_weight, right_gate)], axis=1
    )
    late = lax.all_gather(
        jnp.concatenate([gate_weight.T, final_weight.T], axis=1), "ch", axis=0, tiled=True
    )
    field = jnp.swapaxes(pair_field, 0, 1)

    def message(step):
        part = lax.dynamic_slice(field, (2 * (mine ^ step), 0, 0), (2, 32, 512))
        return jnp.concatenate([part.reshape(64, 512), weights], axis=0)

    got = place([message(0)] + [swap(message(t), t) for t in (1, 2, 3)], mine)
    whole = jnp.swapaxes(got[:, :64].reshape(4, 2, 32, 512), 0, 1).reshape(2, 128, 512)
    wide = got[:, 64:].reshape(128, 4, 128)
    normed = layer_norm(whole.astype(jnp.float32), input_gain, input_bias).astype(jnp.bfloat16)

    def project(weight):
        return jnp.einsum("dc,ack->dak", weight, normed, preferred_element_type=jnp.float32)

    left = jax.nn.sigmoid(project(wide[:, 1])) * project(wide[:, 0])
    right = jax.nn.sigmoid(project(wide[:, 3])) * project(wide[:, 2])
    sent = jnp.concatenate([left.reshape(256, 4, 128), right.reshape(256, 4, 128)], axis=1).astype(
        jnp.bfloat16
    )
    factors = lax.all_to_all(sent, everyone, 0, 0, tiled=True)
    other = swap(factors[:, :4], 1)
    own = factors[:, :4].reshape(256, 512)
    other = other.reshape(256, 512)
    rows = jnp.stack([jnp.where(core == 0, own, other), jnp.where(core == 0, other, own)], axis=1)
    product = jnp.einsum(
        "jk,ik->ji",
        factors[:, 4:].reshape(256, 512),
        rows.reshape(512, 512),
        preferred_element_type=jnp.float32,
    ).astype(jnp.bfloat16)
    gating = jax.nn.sigmoid(
        jnp.einsum("ec,acj->jae", late[:, :128], normed, preferred_element_type=jnp.float32)
    ).astype(jnp.bfloat16)
    sent = jnp.concatenate([product.reshape(256, 4, 128), gating.reshape(256, 4, 128)], axis=1)
    got = lax.all_to_all(sent, everyone, 0, 0, tiled=True)
    hidden = jnp.swapaxes(got[:, :4].reshape(128, 2, 512), 0, 1)
    normed = layer_norm(hidden.astype(jnp.float32), output_gain, output_bias).astype(jnp.bfloat16)
    update = jnp.einsum("ed,jdi->jei", late[:, 128:], normed, preferred_element_type=jnp.float32)
    gating = got[:, 4:].reshape(256, 2, 2, 128).transpose(1, 3, 0, 2).reshape(2, 128, 512)
    update = (update * gating.astype(jnp.float32)).astype(jnp.bfloat16)

    def part(step):
        return lax.dynamic_slice(update, (0, 32 * (mine ^ step), 0), (2, 32, 512))

    got = place([part(0)] + [swap(part(t), t) for t in (1, 2, 3)], mine)
    return jnp.swapaxes(got.reshape(8, 32, 512), 0, 1)


def solution(mesh):
    placed = (
        P("ch", "row", None),
        P(),
        P(),
        P(None, "ch"),
        P(None, "ch"),
        P(None, "ch"),
        P(None, "ch"),
        P(None, "ch"),
        P(),
        P(),
        P(None, "ch"),
    )
    return jax.shard_map(
        body, mesh=mesh, in_specs=placed, out_specs=P("ch", "row", None), check_vma=False
    )
```

profile of v0, /device:TPU:1, one launch (start us, length us, event | category | flops | bytes accessed | tf_op | source)
XLA Modules:
  0.0 90.2 jit_solution(11001124090783543311)
XLA Ops:
  0.0 1.7 %constant_dynamic-slice_fusion.14 = (bf16[32,2,512]{2,1,0:T(2,128)(2,1)S(1)}, bf16[32,2,512]{2,1,0:T(2,128)(2,1)S(1)}, bf16[32,2,512]{2,1,0:T(2,128)(2,1)S(1)}, bf16[32,2,512]{2,1,0:T(2,128)(2,1)S(1)}) fusion(bf16[32,8,512]{2,1,0:T(8,128)(2,1)} %param.11, s32[]{:T(128)S(6)} %select_n.81, s32[]{:T(128)S(6)} %select_n.83, s32[]{:T(128)S(6)} %select_n.82, ...), kind=kLoop, calls=%fused_computation.85 | loop fusion | bytes 524304 | tf_op jit(solution)/shard_map/dynamic-slice
  1.8 0.6 copy-done.1
  2.5 3.3 %collective-permute-start = (bf16[96,512]{1,0:T(8,128)(2,1)S(1)}, bf16[96,512]{1,0:T(8,128)(2,1)S(1)}, u32[]{:S(2)}, u32[]{:S(2)}) collective-permute-start(bf16[96,512]{1,0:T(8,128)(2,1)S(1)} %get-tuple-element.33), channel_id=1, source_target_pairs={{0,1},{1,0},{2,3},{3,2},{4,5},{5,4},{6,7},{7,6},{8,9},{9,8},{10,11... | collective-permute-start | bytes 294920 | tf_op jit(solution)/shard_map/ppermute | solution.py:17
  5.9 1.8 %collective-permute-start.2 = (bf16[96,512]{1,0:T(8,128)(2,1)S(1)}, bf16[96,512]{1,0:T(8,128)(2,1)S(1)}, u32[]{:S(2)}, u32[]{:S(2)}) collective-permute-start(bf16[96,512]{1,0:T(8,128)(2,1)S(1)} %pad_maximum_fusion.13), channel_id=1, source_target_pairs={{0,3},{1,2},{2,1},{3,0},{4,7},{5,6},{6,5},{7,4},{8,11},{9,10},{10,... | collective-permute-start | bytes 294920 | tf_op jit(solution)/shard_map/ppermute | solution.py:17
  7.7 0.7 copy-done.7
  8.4 0.6 copy-done.6
  9.1 1.1 %collective-permute-done.1 = bf16[96,512]{1,0:T(8,128)(2,1)S(1)} collective-permute-done((bf16[96,512]{1,0:T(8,128)(2,1)S(1)}, bf16[96,512]{1,0:T(8,128)(2,1)S(1)}, u32[]{:S(2)}, u32[]{:S(2)}) %collective-permute-start.1) | collective-permute-done | bytes 98336 | tf_op jit(solution)/shard_map/ppermute | solution.py:17
  10.2 2.3 %collective-permute-done.2 = bf16[96,512]{1,0:T(8,128)(2,1)S(1)} collective-permute-done((bf16[96,512]{1,0:T(8,128)(2,1)S(1)}, bf16[96,512]{1,0:T(8,128)(2,1)S(1)}, u32[]{:S(2)}, u32[]{:S(2)}) %collective-permute-start.2) | collective-permute-done | bytes 98336 | tf_op jit(solution)/shard_map/ppermute | solution.py:17
  12.7 0.2 fusion.26
  13.1 0.2 add_convert_fusion.1
  13.3 0.3 fusion.6
  13.6 0.2 fusion.11
  13.8 0.3 copy.64
  14.1 0.2 reshape.143
  14.3 0.3 fusion.9
  14.6 0.2 fusion.10
  14.8 0.3 copy.61
  15.1 0.2 reshape.142
  15.3 1.1 %pad_maximum_fusion = bf16[256,8,128]{2,1,0:T(8,128)(2,1)} fusion(bf16[256,4,128]{2,1,0:T(4,128)(2,1)S(1)} %reshape.143, bf16[256,4,128]{2,1,0:T(4,128)(2,1)S(1)} %reshape.142), kind=kLoop, calls=%fused_computation.22 | loop fusion | flops 1048576 | bytes 1048576 | tf_op jit(solution)/shard_map/concatenate | solution.py:63
  16.3 12.6 %all-to-all-start = ((bf16[256,8,128]{2,1,0:T(8,128)(2,1)}), bf16[256,8,128]{2,1,0:T(8,128)(2,1)S(1)}, u32[]{:S(2)}, u32[]{:S(2)}) async-start(bf16[256,8,128]{2,1,0:T(8,128)(2,1)} %pad_maximum_fusion), calls=%async_computation | async-start | bytes 1048576 | tf_op jit(solution)/shard_map/all_to_all | solution.py:66
  29.0 0.7 copy-done.5
  29.7 7.5 %all_gather.3 = bf16[128,256]{1,0:T(8,128)(2,1)S(1)} all-gather(bf16[32,256]{1,0:T(8,128)(2,1)S(1)} %pad_maximum_fusion.14), channel_id=1, replica_groups=mesh['row'=64,'ch'=4] {'ch'}, dimensions={0}, use_global_device_ids=true | all-gather | bytes 81920 | tf_op jit(solution)/shard_map/all_gather | solution.py:44
  37.2 12.9 %all-to-all-done = bf16[256,8,128]{2,1,0:T(8,128)(2,1)S(1)} async-done(((bf16[256,8,128]{2,1,0:T(8,128)(2,1)}), bf16[256,8,128]{2,1,0:T(8,128)(2,1)S(1)}, u32[]{:S(2)}, u32[]{:S(2)}) %all-to-all-start) | async-done | bytes 524320 | tf_op jit(solution)/shard_map/all_to_all | solution.py:66
  50.1 0.3 collective-permute-start.3
  50.4 0.2 fusion.18
  50.6 0.3 fusion.14
  51.0 0.3 copy.69
  51.3 0.5 collective-permute-done.3
  51.7 0.3 broadcast_select_fusion.1
  52.1 0.1 select_n.99
  52.4 1.2 %pad_maximum_fusion.1 = bf16[256,2,512]{2,1,0:T(2,128)(2,1)S(1)} fusion(bf16[256,1,512]{2,1,0:T(2,128)(2,1)S(1)} %select_n.100, bf16[256,1,512]{2,1,0:T(2,128)(2,1)S(1)} %select_n.99), kind=kLoop, calls=%fused_computation.23 | loop fusion | flops 1048576 | bytes 1048576 | tf_op jit(solution)/shard_map/stack | solution.py:70
  53.6 0.2 reshape.145
  53.8 0.3 convolution_convert_fusion
  54.2 1.1 %pad_maximum_fusion.2 = bf16[256,8,128]{2,1,0:T(8,128)(2,1)} fusion(bf16[256,4,128]{2,1,0:T(4,128)(2,1)S(1)} %bitcast.119, bf16[256,4,128]{2,1,0:T(4,128)(2,1)S(1)} %reshape.146), kind=kLoop, calls=%fused_computation.24 | loop fusion | flops 1048576 | bytes 1048576 | tf_op jit(solution)/shard_map/concatenate | solution.py:80
  55.3 5.3 %all-to-all-start.1 = ((bf16[256,8,128]{2,1,0:T(8,128)(2,1)}), bf16[256,8,128]{2,1,0:T(8,128)(2,1)S(1)}, u32[]{:S(2)}, u32[]{:S(2)}) async-start(bf16[256,8,128]{2,1,0:T(8,128)(2,1)} %pad_maximum_fusion.2), calls=%async_computation.1 | async-start | bytes 1048576 | tf_op jit(solution)/shard_map/all_to_all | solution.py:81
  60.7 21.1 %all-to-all-done.1 = bf16[256,8,128]{2,1,0:T(8,128)(2,1)S(1)} async-done(((bf16[256,8,128]{2,1,0:T(8,128)(2,1)}), bf16[256,8,128]{2,1,0:T(8,128)(2,1)S(1)}, u32[]{:S(2)}, u32[]{:S(2)}) %all-to-all-start.1) | async-done | bytes 524320 | tf_op jit(solution)/shard_map/all_to_all | solution.py:81
  81.8 0.1 slice_convert_fusion.1
  81.9 0.4 reshape.151
  82.3 0.2 copy.71
  82.5 0.2 copy.72
  83.0 0.6 copy-done.8
  83.6 0.3 fusion.13
  83.9 0.6 collective-permute-start.6
  84.5 1.1 %collective-permute-start.5 = (bf16[2,32,512]{2,1,0:T(8,128)(2,1)S(1)}, bf16[2,32,512]{2,1,0:T(8,128)(2,1)S(1)}, u32[]{:S(2)}, u32[]{:S(2)}) collective-permute-start(bf16[2,32,512]{2,1,0:T(8,128)(2,1)S(1)} %get-tuple-element.22), channel_id=1, source_target_pairs={{0,2},{1,3},{2,0},{3,1},{4,6},{5,7},{6,4},{7,5},{8,10},{9,11},{10,... | collective-permute-start | bytes 196616 | tf_op jit(solution)/shard_map/ppermute | solution.py:17
  85.6 0.6 collective-permute-start.4
  86.2 2.2 %collective-permute-done.6 = bf16[2,32,512]{2,1,0:T(8,128)(2,1)S(1)} collective-permute-done((bf16[2,32,512]{2,1,0:T(8,128)(2,1)S(1)}, bf16[2,32,512]{2,1,0:T(8,128)(2,1)S(1)}, u32[]{:S(2)}, u32[]{:S(2)}) %collective-permute-start.6) | collective-permute-done | bytes 65568 | tf_op jit(solution)/shard_map/ppermute | solution.py:17
  88.3 0.9 %collective-permute-done.5 = bf16[2,32,512]{2,1,0:T(8,128)(2,1)S(1)} collective-permute-done((bf16[2,32,512]{2,1,0:T(8,128)(2,1)S(1)}, bf16[2,32,512]{2,1,0:T(8,128)(2,1)S(1)}, u32[]{:S(2)}, u32[]{:S(2)}) %collective-permute-start.5) | collective-permute-done | bytes 65568 | tf_op jit(solution)/shard_map/ppermute | solution.py:17
  89.4 0.9 copy.101
  (49 shorter events, 1.4 us)
Async XLA Ops:
  1.7 0.7 copy-start.1
  1.7 0.7 copy-start.2
  1.7 0.7 copy-start.3
  1.8 0.7 copy-start
  2.5 6.6 %collective-permute-start = (bf16[96,512]{1,0:T(8,128)(2,1)S(1)}, bf16[96,512]{1,0:T(8,128)(2,1)S(1)}, u32[]{:S(2)}, u32[]{:S(2)}) collective-permute-start(bf16[96,512]{1,0:T(8,128)(2,1)S(1)} %get-tuple-element.33), channel_id=1, source_target_pairs={{0,1},{1,0},{2,3},{3,2},{4,5},{5,4},{6,7},{7,6},{8,9},{9,8},{10,11... | collective-permute-start | bytes 294920 | tf_op jit(solution)/shard_map/ppermute | solution.py:17
  5.8 4.4 %collective-permute-start.1 = (bf16[96,512]{1,0:T(8,128)(2,1)S(1)}, bf16[96,512]{1,0:T(8,128)(2,1)S(1)}, u32[]{:S(2)}, u32[]{:S(2)}) collective-permute-start(bf16[96,512]{1,0:T(8,128)(2,1)S(1)} %get-tuple-element.34), channel_id=1, source_target_pairs={{0,2},{1,3},{2,0},{3,1},{4,6},{5,7},{6,4},{7,5},{8,10},{9,11},{10,... | collective-permute-start | bytes 294920 | tf_op jit(solution)/shard_map/ppermute | solution.py:17
  5.9 6.6 %collective-permute-start.2 = (bf16[96,512]{1,0:T(8,128)(2,1)S(1)}, bf16[96,512]{1,0:T(8,128)(2,1)S(1)}, u32[]{:S(2)}, u32[]{:S(2)}) collective-permute-start(bf16[96,512]{1,0:T(8,128)(2,1)S(1)} %pad_maximum_fusion.13), channel_id=1, source_target_pairs={{0,3},{1,2},{2,1},{3,0},{4,7},{5,6},{6,5},{7,4},{8,11},{9,10},{10,... | collective-permute-start | bytes 294920 | tf_op jit(solution)/shard_map/ppermute | solution.py:17
  7.7 0.7 copy-start.7
  8.3 0.7 copy-start.6
  16.3 33.7 %all-to-all-start = ((bf16[256,8,128]{2,1,0:T(8,128)(2,1)}), bf16[256,8,128]{2,1,0:T(8,128)(2,1)S(1)}, u32[]{:S(2)}, u32[]{:S(2)}) async-start(bf16[256,8,128]{2,1,0:T(8,128)(2,1)} %pad_maximum_fusion), calls=%async_computation | async-start | bytes 1048576 | tf_op jit(solution)/shard_map/all_to_all | solution.py:66
  29.0 0.7 copy-start.5
  29.0 0.7 copy-start.4
  50.1 1.6 %collective-permute-start.3 = (bf16[256,4,128]{2,1,0:T(4,128)(2,1)S(1)}, bf16[256,4,128]{2,1,0:T(4,128)(2,1)S(1)}, u32[]{:S(2)}, u32[]{:S(2)}) collective-permute-start(bf16[256,4,128]{2,1,0:T(4,128)(2,1)S(1)} %slice.55), channel_id=1, source_target_pairs={{0,1},{1,0},{2,3},{3,2},{4,5},{5,4},{6,7},{7,6},{8,9},{9,8},{10,11... | collective-permute-start | bytes 786440 | tf_op jit(solution)/shard_map/ppermute | solution.py:17
  55.3 26.5 %all-to-all-start.1 = ((bf16[256,8,128]{2,1,0:T(8,128)(2,1)}), bf16[256,8,128]{2,1,0:T(8,128)(2,1)S(1)}, u32[]{:S(2)}, u32[]{:S(2)}) async-start(bf16[256,8,128]{2,1,0:T(8,128)(2,1)} %pad_maximum_fusion.2), calls=%async_computation.1 | async-start | bytes 1048576 | tf_op jit(solution)/shard_map/all_to_all | solution.py:81
  82.9 0.7 copy-start.8
  82.9 0.7 copy-start.9
  83.9 4.4 %collective-permute-start.6 = (bf16[2,32,512]{2,1,0:T(8,128)(2,1)S(1)}, bf16[2,32,512]{2,1,0:T(8,128)(2,1)S(1)}, u32[]{:S(2)}, u32[]{:S(2)}) collective-permute-start(bf16[2,32,512]{2,1,0:T(8,128)(2,1)S(1)} %get-tuple-element.21), channel_id=1, source_target_pairs={{0,3},{1,2},{2,1},{3,0},{4,7},{5,6},{6,5},{7,4},{8,11},{9,10},{10,... | collective-permute-start | bytes 196616 | tf_op jit(solution)/shard_map/ppermute | solution.py:17
  84.5 4.8 %collective-permute-start.5 = (bf16[2,32,512]{2,1,0:T(8,128)(2,1)S(1)}, bf16[2,32,512]{2,1,0:T(8,128)(2,1)S(1)}, u32[]{:S(2)}, u32[]{:S(2)}) collective-permute-start(bf16[2,32,512]{2,1,0:T(8,128)(2,1)S(1)} %get-tuple-element.22), channel_id=1, source_target_pairs={{0,2},{1,3},{2,0},{3,1},{4,6},{5,7},{6,4},{7,5},{8,10},{9,11},{10,... | collective-permute-start | bytes 196616 | tf_op jit(solution)/shard_map/ppermute | solution.py:17
  85.6 3.7 %collective-permute-start.4 = (bf16[2,32,512]{2,1,0:T(8,128)(2,1)S(1)}, bf16[2,32,512]{2,1,0:T(8,128)(2,1)S(1)}, u32[]{:S(2)}, u32[]{:S(2)}) collective-permute-start(bf16[2,32,512]{2,1,0:T(8,128)(2,1)S(1)} %get-tuple-element.23), channel_id=1, source_target_pairs={{0,1},{1,0},{2,3},{3,2},{4,5},{5,4},{6,7},{7,6},{8,9},{9,8},{10,11... | collective-permute-start | bytes 196616 | tf_op jit(solution)/shard_map/ppermute | solution.py:17
where the time goes:
time: 90.7 us; the launch traced here: 90.2 us
  waiting for transfers between devices  40.9 us (45%)
  starting transfers between devices  25.6 us (28%)
  local copies, waits for them, and re-layouts  8.92 us (10%)
  blocking collectives  7.46 us (8%)
  other arithmetic  4.84 us (5%)
  matrix products  1.97 us (2%)
    all_to_all x1, waiting for transfers between devices, body(): got = lax.all_to_all(sent, everyone, 0, 0, tiled=True)  21.1 us
    all_to_all x1, waiting for transfers between devices, body(): factors = lax.all_to_all(sent, everyone, 0, 0, tiled=True)  12.9 us
    all_to_all x1, starting transfers between devices, body(): factors = lax.all_to_all(sent, everyone, 0, 0, tiled=True)  12.6 us
    ppermute x7, starting transfers between devices, swap(): return lax.ppermute(array, 'ch', [(s, s ^ step) for s in range(4)])  7.68 us
    all_gather x1, blocking collectives, body(): lax.all_gather(jnp.concatenate([gate_weight.T, final_weight.T], axis=1),...  7.46 us
    ppermute x7, waiting for transfers between devices, swap(): return lax.ppermute(array, 'ch', [(s, s ^ step) for s in range(4)])  6.98 us
    all_to_all x1, starting transfers between devices, body(): got = lax.all_to_all(sent, everyone, 0, 0, tiled=True)  5.33 us
    unnamed x24, local copies, waits for them, and re-layouts  3.31 us
  transfers between devices with their start and end apart: 9, of which 7 were waited for; matrix products, arithmetic and copies ran while one was open for 1% of the time, Pallas kernels for 0%

commit v1 on v0

--- a/solution.py
+++ b/solution.py
@@ -41,9 +41,11 @@
     weights = jnp.concatenate(
         [w.T for w in (left_weight, left_gate, right_weight, right_gate)], axis=1
     )
-    late = lax.all_gather(
-        jnp.concatenate([gate_weight.T, final_weight.T], axis=1), "ch", axis=0, tiled=True
-    )
+    block = jnp.concatenate([gate_weight.T, final_weight.T], axis=1)
+    devices = lax.axis_size("ch")
+    pieces = jnp.stack([block for _ in range(devices)])
+    pieces = lax.all_to_all(pieces, "ch", split_axis=0, concat_axis=0)
+    late = jnp.concatenate(pieces, axis=0)
     field = jnp.swapaxes(pair_field, 0, 1)
 
     def message(step):

time: 90.7 us -> 97.7 us (1.077)
  waiting for transfers between devices: 40.9 us -> 50.8 us
  blocking collectives: 7.46 us -> 0 us
  starting transfers between devices: 25.6 us -> 29.5 us
    all_gather x1 -> x0, blocking collectives: 7.46 us -> none  [body(): lax.all_gather(jnp.concatenate([gate_weight.T, final_weight.T], axis=1),...]
    all_to_all x1, waiting for transfers between devices: 12.9 us -> 20.3 us  [body(): factors = lax.all_to_all(sent, everyone, 0, 0, tiled=True)]
    all_to_all x0 -> x1, starting transfers between devices: none -> 3.48 us  [body(): pieces = lax.all_to_all(pieces, 'ch', split_axis=0, concat_axis=0)]
    all_to_all x0 -> x1, waiting for transfers between devices: none -> 2.85 us  [body(): pieces = lax.all_to_all(pieces, 'ch', split_axis=0, concat_axis=0)]
    another operation x3 -> x4, local copies, waits for them, and re-layouts: 2.22 us -> 2.85 us
  transfers between devices with their start and end apart: 9 -> 10, of which waited for: 7 -> 7; matrix products, arithmetic and copies ran while one was open for 1% -> 1% of each run, Pallas kernels for 0% -> 0%
where the time goes in v1:
time: 97.7 us; the launch traced here: 97.2 us
  waiting for transfers between devices  50.8 us (52%)
  starting transfers between devices  29.5 us (30%)
  local copies, waits for them, and re-layouts  9.56 us (10%)
  other arithmetic  4.82 us (5%)
  matrix products  1.98 us (2%)
    all_to_all x1, waiting for transfers between devices, body(): got = lax.all_to_all(sent, everyone, 0, 0, tiled=True)  21.2 us
    all_to_all x1, waiting for transfers between devices, body(): factors = lax.all_to_all(sent, everyone, 0, 0, tiled=True)  20.3 us
    all_to_all x1, starting transfers between devices, body(): factors = lax.all_to_all(sent, everyone, 0, 0, tiled=True)  12.6 us
    ppermute x7, starting transfers between devices, swap(): return lax.ppermute(array, 'ch', [(s, s ^ step) for s in range(4)])  7.5 us
    ppermute x7, waiting for transfers between devices, swap(): return lax.ppermute(array, 'ch', [(s, s ^ step) for s in range(4)])  6.5 us
    all_to_all x1, starting transfers between devices, body(): got = lax.all_to_all(sent, everyone, 0, 0, tiled=True)  5.89 us
    all_to_all x1, starting transfers between devices, body(): pieces = lax.all_to_all(pieces, 'ch', split_axis=0, concat_axis=0)  3.48 us
    unnamed x24, local copies, waits for them, and re-layouts  3.31 us
  transfers between devices with their start and end apart: 10, of which 7 were waited for; matrix products, arithmetic and copies ran while one was open for 1% of the time, Pallas kernels for 0%

profile of v1, /device:TPU:1, one launch (start us, length us, event | category | flops | bytes accessed | tf_op | source)
XLA Modules:
  0.0 97.2 jit_solution(15726027051890271585)
XLA Ops:
  0.0 1.7 %constant_dynamic-slice_fusion.14 = (bf16[32,2,512]{2,1,0:T(2,128)(2,1)S(1)}, bf16[32,2,512]{2,1,0:T(2,128)(2,1)S(1)}, bf16[32,2,512]{2,1,0:T(2,128)(2,1)S(1)}, bf16[32,2,512]{2,1,0:T(2,128)(2,1)S(1)}) fusion(bf16[32,8,512]{2,1,0:T(8,128)(2,1)} %param.11, s32[]{:T(128)S(6)} %select_n.81, s32[]{:T(128)S(6)} %select_n.83, s32[]{:T(128)S(6)} %select_n.82, ...), kind=kLoop, calls=%fused_computation.85 | loop fusion | bytes 524304 | tf_op jit(solution)/shard_map/dynamic-slice
  1.8 0.6 copy-done.1
  2.5 3.3 %collective-permute-start = (bf16[96,512]{1,0:T(8,128)(2,1)S(1)}, bf16[96,512]{1,0:T(8,128)(2,1)S(1)}, u32[]{:S(2)}, u32[]{:S(2)}) collective-permute-start(bf16[96,512]{1,0:T(8,128)(2,1)S(1)} %get-tuple-element.33), channel_id=1, source_target_pairs={{0,1},{1,0},{2,3},{3,2},{4,5},{5,4},{6,7},{7,6},{8,9},{9,8},{10,11... | collective-permute-start | bytes 294920 | tf_op jit(solution)/shard_map/ppermute | solution.py:17
  5.9 1.8 %collective-permute-start.2 = (bf16[96,512]{1,0:T(8,128)(2,1)S(1)}, bf16[96,512]{1,0:T(8,128)(2,1)S(1)}, u32[]{:S(2)}, u32[]{:S(2)}) collective-permute-start(bf16[96,512]{1,0:T(8,128)(2,1)S(1)} %pad_maximum_fusion.13), channel_id=1, source_target_pairs={{0,3},{1,2},{2,1},{3,0},{4,7},{5,6},{6,5},{7,4},{8,11},{9,10},{10,... | collective-permute-start | bytes 294920 | tf_op jit(solution)/shard_map/ppermute | solution.py:17
  7.7 0.7 copy-done.7
  8.4 0.6 copy-done.6
  9.1 1.1 %collective-permute-done.1 = bf16[96,512]{1,0:T(8,128)(2,1)S(1)} collective-permute-done((bf16[96,512]{1,0:T(8,128)(2,1)S(1)}, bf16[96,512]{1,0:T(8,128)(2,1)S(1)}, u32[]{:S(2)}, u32[]{:S(2)}) %collective-permute-start.1) | collective-permute-done | bytes 98336 | tf_op jit(solution)/shard_map/ppermute | solution.py:17
  10.2 2.3 %collective-permute-done.2 = bf16[96,512]{1,0:T(8,128)(2,1)S(1)} collective-permute-done((bf16[96,512]{1,0:T(8,128)(2,1)S(1)}, bf16[96,512]{1,0:T(8,128)(2,1)S(1)}, u32[]{:S(2)}, u32[]{:S(2)}) %collective-permute-start.2) | collective-permute-done | bytes 98336 | tf_op jit(solution)/shard_map/ppermute | solution.py:17
  12.7 0.2 fusion.26
  13.1 0.2 add_convert_fusion.1
  13.3 0.3 fusion.6
  13.6 0.2 fusion.11
  13.8 0.3 copy.64
  14.1 0.2 reshape.148
  14.3 0.3 fusion.9
  14.6 0.2 fusion.10
  14.8 0.3 copy.61
  15.1 0.2 reshape.147
  15.3 1.1 %pad_maximum_fusion = bf16[256,8,128]{2,1,0:T(8,128)(2,1)} fusion(bf16[256,4,128]{2,1,0:T(4,128)(2,1)S(1)} %reshape.148, bf16[256,4,128]{2,1,0:T(4,128)(2,1)S(1)} %reshape.147), kind=kLoop, calls=%fused_computation.22 | loop fusion | flops 1048576 | bytes 1048576 | tf_op jit(solution)/shard_map/concatenate | solution.py:65
  16.3 12.6 %all-to-all-start = ((bf16[256,8,128]{2,1,0:T(8,128)(2,1)}), bf16[256,8,128]{2,1,0:T(8,128)(2,1)S(1)}, u32[]{:S(2)}, u32[]{:S(2)}) async-start(bf16[256,8,128]{2,1,0:T(8,128)(2,1)} %pad_maximum_fusion), calls=%async_computation | async-start | bytes 1048576 | tf_op jit(solution)/shard_map/all_to_all | solution.py:68
  29.0 0.7 copy-done.5
  29.7 20.3 %all-to-all-done = bf16[256,8,128]{2,1,0:T(8,128)(2,1)S(1)} async-done(((bf16[256,8,128]{2,1,0:T(8,128)(2,1)}), bf16[256,8,128]{2,1,0:T(8,128)(2,1)S(1)}, u32[]{:S(2)}, u32[]{:S(2)}) %all-to-all-start) | async-done | bytes 524320 | tf_op jit(solution)/shard_map/all_to_all | solution.py:68
  50.0 0.6 stack.63
  50.7 3.5 %all-to-all-start.1 = ((bf16[4,32,256]{2,1,0:T(8,128)(2,1)}), bf16[4,32,256]{2,1,0:T(8,128)(2,1)S(1)}, u32[]{:S(2)}, u32[]{:S(2)}) async-start(bf16[4,32,256]{2,1,0:T(8,128)(2,1)} %stack.63), calls=%async_computation.1 | async-start | bytes 131072 | tf_op jit(solution)/shard_map/all_to_all | solution.py:47
  54.4 0.2 fusion.18
  54.6 2.8 %all-to-all-done.1 = bf16[4,32,256]{2,1,0:T(8,128)(2,1)S(1)} async-done(((bf16[4,32,256]{2,1,0:T(8,128)(2,1)}), bf16[4,32,256]{2,1,0:T(8,128)(2,1)S(1)}, u32[]{:S(2)}, u32[]{:S(2)}) %all-to-all-start.1) | async-done | bytes 65568 | tf_op jit(solution)/shard_map/all_to_all | solution.py:47
  57.4 0.3 fusion.14
  57.8 0.3 copy.69
  58.0 0.3 broadcast_select_fusion.1
  58.4 0.1 select_n.99
  58.7 1.2 %pad_maximum_fusion.1 = bf16[256,2,512]{2,1,0:T(2,128)(2,1)S(1)} fusion(bf16[256,1,512]{2,1,0:T(2,128)(2,1)S(1)} %select_n.100, bf16[256,1,512]{2,1,0:T(2,128)(2,1)S(1)} %select_n.99), kind=kLoop, calls=%fused_computation.23 | loop fusion | flops 1048576 | bytes 1048576 | tf_op jit(solution)/shard_map/stack | solution.py:72
  59.9 0.2 reshape.150
  60.1 0.3 convolution_convert_fusion
  60.5 1.1 %pad_maximum_fusion.2 = bf16[256,8,128]{2,1,0:T(8,128)(2,1)} fusion(bf16[256,4,128]{2,1,0:T(4,128)(2,1)S(1)} %bitcast.120, bf16[256,4,128]{2,1,0:T(4,128)(2,1)S(1)} %reshape.151), kind=kLoop, calls=%fused_computation.24 | loop fusion | flops 1048576 | bytes 1048576 | tf_op jit(solution)/shard_map/concatenate | solution.py:82
  61.6 5.9 %all-to-all-start.2 = ((bf16[256,8,128]{2,1,0:T(8,128)(2,1)}), bf16[256,8,128]{2,1,0:T(8,128)(2,1)S(1)}, u32[]{:S(2)}, u32[]{:S(2)}) async-start(bf16[256,8,128]{2,1,0:T(8,128)(2,1)} %pad_maximum_fusion.2), calls=%async_computation.2 | async-start | bytes 1048576 | tf_op jit(solution)/shard_map/all_to_all | solution.py:83
  67.5 21.2 %all-to-all-done.2 = bf16[256,8,128]{2,1,0:T(8,128)(2,1)S(1)} async-done(((bf16[256,8,128]{2,1,0:T(8,128)(2,1)}), bf16[256,8,128]{2,1,0:T(8,128)(2,1)S(1)}, u32[]{:S(2)}, u32[]{:S(2)}) %all-to-all-start.2) | async-done | bytes 524320 | tf_op jit(solution)/shard_map/all_to_all | solution.py:83
  88.7 0.1 slice_convert_fusion.1
  88.8 0.4 reshape.157
  89.2 0.2 copy.71
  89.4 0.2 copy.72
  89.9 0.6 copy-done.8
  90.5 0.3 fusion.13
  90.9 0.6 collective-permute-start.6
  91.4 1.1 %collective-permute-start.5 = (bf16[2,32,512]{2,1,0:T(8,128)(2,1)S(1)}, bf16[2,32,512]{2,1,0:T(8,128)(2,1)S(1)}, u32[]{:S(2)}, u32[]{:S(2)}) collective-permute-start(bf16[2,32,512]{2,1,0:T(8,128)(2,1)S(1)} %get-tuple-element.22), channel_id=1, source_target_pairs={{0,2},{1,3},{2,0},{3,1},{4,6},{5,7},{6,4},{7,5},{8,10},{9,11},{10,... | collective-permute-start | bytes 196616 | tf_op jit(solution)/shard_map/ppermute | solution.py:17
  92.5 0.6 collective-permute-start.4
  93.1 2.2 %collective-permute-done.6 = bf16[2,32,512]{2,1,0:T(8,128)(2,1)S(1)} collective-permute-done((bf16[2,32,512]{2,1,0:T(8,128)(2,1)S(1)}, bf16[2,32,512]{2,1,0:T(8,128)(2,1)S(1)}, u32[]{:S(2)}, u32[]{:S(2)}) %collective-permute-start.6) | collective-permute-done | bytes 65568 | tf_op jit(solution)/shard_map/ppermute | solution.py:17
  95.3 0.9 collective-permute-done.5
  96.3 0.9 copy.101
  (51 shorter events, 1.5 us)
Async XLA Ops:
  1.7 0.7 copy-start.1
  1.7 0.7 copy-start.2
  1.7 0.7 copy-start.3
  1.8 0.7 copy-start
  2.5 6.6 %collective-permute-start = (bf16[96,512]{1,0:T(8,128)(2,1)S(1)}, bf16[96,512]{1,0:T(8,128)(2,1)S(1)}, u32[]{:S(2)}, u32[]{:S(2)}) collective-permute-start(bf16[96,512]{1,0:T(8,128)(2,1)S(1)} %get-tuple-element.33), channel_id=1, source_target_pairs={{0,1},{1,0},{2,3},{3,2},{4,5},{5,4},{6,7},{7,6},{8,9},{9,8},{10,11... | collective-permute-start | bytes 294920 | tf_op jit(solution)/shard_map/ppermute | solution.py:17
  5.8 4.4 %collective-permute-start.1 = (bf16[96,512]{1,0:T(8,128)(2,1)S(1)}, bf16[96,512]{1,0:T(8,128)(2,1)S(1)}, u32[]{:S(2)}, u32[]{:S(2)}) collective-permute-start(bf16[96,512]{1,0:T(8,128)(2,1)S(1)} %get-tuple-element.34), channel_id=1, source_target_pairs={{0,2},{1,3},{2,0},{3,1},{4,6},{5,7},{6,4},{7,5},{8,10},{9,11},{10,... | collective-permute-start | bytes 294920 | tf_op jit(solution)/shard_map/ppermute | solution.py:17
  5.9 6.6 %collective-permute-start.2 = (bf16[96,512]{1,0:T(8,128)(2,1)S(1)}, bf16[96,512]{1,0:T(8,128)(2,1)S(1)}, u32[]{:S(2)}, u32[]{:S(2)}) collective-permute-start(bf16[96,512]{1,0:T(8,128)(2,1)S(1)} %pad_maximum_fusion.13), channel_id=1, source_target_pairs={{0,3},{1,2},{2,1},{3,0},{4,7},{5,6},{6,5},{7,4},{8,11},{9,10},{10,... | collective-permute-start | bytes 294920 | tf_op jit(solution)/shard_map/ppermute | solution.py:17
  7.7 0.7 copy-start.7
  8.3 0.7 copy-start.6
  16.3 33.7 %all-to-all-start = ((bf16[256,8,128]{2,1,0:T(8,128)(2,1)}), bf16[256,8,128]{2,1,0:T(8,128)(2,1)S(1)}, u32[]{:S(2)}, u32[]{:S(2)}) async-start(bf16[256,8,128]{2,1,0:T(8,128)(2,1)} %pad_maximum_fusion), calls=%async_computation | async-start | bytes 1048576 | tf_op jit(solution)/shard_map/all_to_all | solution.py:68
  29.0 0.7 copy-start.5
  29.0 0.7 copy-start.4
  50.7 6.7 %all-to-all-start.1 = ((bf16[4,32,256]{2,1,0:T(8,128)(2,1)}), bf16[4,32,256]{2,1,0:T(8,128)(2,1)S(1)}, u32[]{:S(2)}, u32[]{:S(2)}) async-start(bf16[4,32,256]{2,1,0:T(8,128)(2,1)} %stack.63), calls=%async_computation.1 | async-start | bytes 131072 | tf_op jit(solution)/shard_map/all_to_all | solution.py:47
  54.2 3.8 %collective-permute-start.3 = (bf16[256,4,128]{2,1,0:T(4,128)(2,1)S(1)}, bf16[256,4,128]{2,1,0:T(4,128)(2,1)S(1)}, u32[]{:S(2)}, u32[]{:S(2)}) collective-permute-start(bf16[256,4,128]{2,1,0:T(4,128)(2,1)S(1)} %slice.55), channel_id=1, source_target_pairs={{0,1},{1,0},{2,3},{3,2},{4,5},{5,4},{6,7},{7,6},{8,9},{9,8},{10,11... | collective-permute-start | bytes 786440 | tf_op jit(solution)/shard_map/ppermute | solution.py:17
  61.6 27.1 %all-to-all-start.2 = ((bf16[256,8,128]{2,1,0:T(8,128)(2,1)}), bf16[256,8,128]{2,1,0:T(8,128)(2,1)S(1)}, u32[]{:S(2)}, u32[]{:S(2)}) async-start(bf16[256,8,128]{2,1,0:T(8,128)(2,1)} %pad_maximum_fusion.2), calls=%async_computation.2 | async-start | bytes 1048576 | tf_op jit(solution)/shard_map/all_to_all | solution.py:83
  89.8 0.7 copy-start.8
  89.8 0.7 copy-start.9
  90.9 4.4 %collective-permute-start.6 = (bf16[2,32,512]{2,1,0:T(8,128)(2,1)S(1)}, bf16[2,32,512]{2,1,0:T(8,128)(2,1)S(1)}, u32[]{:S(2)}, u32[]{:S(2)}) collective-permute-start(bf16[2,32,512]{2,1,0:T(8,128)(2,1)S(1)} %get-tuple-element.21), channel_id=1, source_target_pairs={{0,3},{1,2},{2,1},{3,0},{4,7},{5,6},{6,5},{7,4},{8,11},{9,10},{10,... | collective-permute-start | bytes 196616 | tf_op jit(solution)/shard_map/ppermute | solution.py:17
  91.4 4.8 %collective-permute-start.5 = (bf16[2,32,512]{2,1,0:T(8,128)(2,1)S(1)}, bf16[2,32,512]{2,1,0:T(8,128)(2,1)S(1)}, u32[]{:S(2)}, u32[]{:S(2)}) collective-permute-start(bf16[2,32,512]{2,1,0:T(8,128)(2,1)S(1)} %get-tuple-element.22), channel_id=1, source_target_pairs={{0,2},{1,3},{2,0},{3,1},{4,6},{5,7},{6,4},{7,5},{8,10},{9,11},{10,... | collective-permute-start | bytes 196616 | tf_op jit(solution)/shard_map/ppermute | solution.py:17
  92.5 3.7 %collective-permute-start.4 = (bf16[2,32,512]{2,1,0:T(8,128)(2,1)S(1)}, bf16[2,32,512]{2,1,0:T(8,128)(2,1)S(1)}, u32[]{:S(2)}, u32[]{:S(2)}) collective-permute-start(bf16[2,32,512]{2,1,0:T(8,128)(2,1)S(1)} %get-tuple-element.23), channel_id=1, source_target_pairs={{0,1},{1,0},{2,3},{3,2},{4,5},{5,4},{6,7},{7,6},{8,9},{9,8},{10,11... | collective-permute-start | bytes 196616 | tf_op jit(solution)/shard_map/ppermute | solution.py:17
